TPU v7x, 128 devices: a whole 4x4x4 slice. The times are simulated.
128 devices in a mesh: row: 8 (over y, core), col: 16 (over z, x).
Axes of the slice: x: 4, y: 4, z: 4, core: 2. Of those that a mesh axis runs over, the one named last changes fastest.
Arguments:
- tokens: bfloat16 [65536, 768], P(('row', 'col')), may hold values from -6 to 6
- expert_ids: int32 [65536, 1], P(('row', 'col')), may hold values from 0 to 127
- gate_values: float32 [65536], P(('row', 'col')), may hold values from 0.2 to 1
- weight_in: bfloat16 [128, 768, 3072], P(('row', 'col')), may hold values from -0.21875 to 0.21875
- weight_out: bfloat16 [128, 3072, 768], P(('row', 'col')), may hold values from -0.109375 to 0.109375
- cotangent: bfloat16 [65536, 768], P(('row', 'col')), may hold values from -6 to 6
Outputs:
- expert_out: bfloat16 [65536, 768], P(('row', 'col'))
- grad_tokens: bfloat16 [65536, 768], P(('row', 'col'))
- grad_gates: float32 [65536], P(('row', 'col'))
- grad_w_in: bfloat16 [128, 768, 3072], P(('row', 'col'))
- grad_w_out: bfloat16 [128, 3072, 768], P(('row', 'col'))
All inputs are finite; a program needn't handle non-finite values.
Results may differ from a plain program's by a relative error of at most 0.0058.
Values may be sent and summed in bfloat16 or wider, within the bound.
No kernel may reach another device: no remote copies, remote signals or barrier semaphores. Data moves between devices by JAX's collectives and lax.ppermute only.
A program may use at most 128 MiB of HBM per device.

v0:
```python
import jax
import jax.numpy as jnp
from jax import lax
from jax.sharding import PartitionSpec as P


def body(tokens, expert_ids, gate_values, weight_in, weight_out, cotangent):
    tok_dev, model_width = tokens.shape
    exp_dev = weight_in.shape[0]
    row_count = lax.axis_size("row")
    col_count = lax.axis_size("col")
    groups = row_count * col_count
    experts = exp_dev * groups
    capacity = max(2, (5 * tok_dev + 4 * experts - 1) // (4 * experts))
    routed = expert_ids[:, 0]
    one_hot = (routed[:, None] == jnp.arange(experts, dtype=jnp.int32)[None, :]).astype(jnp.int32)
    before = jnp.cumsum(one_hot, axis=0) - one_hot
    slot_rank = jnp.sum(before * one_hot, axis=1)
    position = jnp.where(slot_rank < capacity, routed * capacity + slot_rank, experts * capacity)
    scaled = (gate_values[:, None] * cotangent.astype(jnp.float32)).astype(jnp.bfloat16)

    def place_rows(source):
        filled = (
            jnp.zeros((experts * capacity, model_width), source.dtype)
            .at[position]
            .set(source, mode="drop")
        )
        return filled.reshape(groups, exp_dev, capacity, model_width)

    def pick_rows(source):
        flat_rows = source.reshape(experts * capacity, model_width)
        return jnp.take(flat_rows, position, axis=0, mode="fill", fill_value=0)

    def outward(stacked):
        arrived = lax.all_to_all(stacked, ("row", "col"), split_axis=0, concat_axis=0, tiled=True)
        return arrived

    def inward(stacked):
        arrived = lax.all_to_all(stacked, ("row", "col"), split_axis=0, concat_axis=0, tiled=True)
        return arrived

    sent_rows = outward(place_rows(tokens)[:, None])[:, 0]
    pre_act = jnp.einsum("sjcd,jdf->sjcf", sent_rows, weight_in, preferred_element_type=jnp.float32)
    act_rows = jax.nn.gelu(pre_act).astype(jnp.bfloat16)
    out_rows = jnp.einsum(
        "sjcf,jfd->sjcd", act_rows, weight_out, preferred_element_type=jnp.float32
    ).astype(jnp.bfloat16)
    pre_act, act_rows, out_rows = (pre_act, act_rows, out_rows)
    ffn_rows = pick_rows(inward(out_rows[:, None])[:, 0])
    sent_cot = outward(place_rows(scaled)[:, None])[:, 0]
    grad_act = jnp.einsum(
        "sjcd,jfd->sjcf", sent_cot, weight_out, preferred_element_type=jnp.float32
    )
    unused, pull_back = jax.vjp(jax.nn.gelu, pre_act)
    grad_pre = pull_back(grad_act)[0].astype(jnp.bfloat16)
    grad_out = jnp.einsum(
        "sjcf,sjcd->jfd", act_rows, sent_cot, preferred_element_type=jnp.float32
    ).astype(jnp.bfloat16)
    grad_in = jnp.einsum(
        "sjcd,sjcf->jdf", sent_rows, grad_pre, preferred_element_type=jnp.float32
    ).astype(jnp.bfloat16)
    back_rows = jnp.einsum(
        "sjcf,jdf->sjcd", grad_pre, weight_in, preferred_element_type=jnp.float32
    ).astype(jnp.bfloat16)
    back_rows, grad_in, grad_out = (back_rows, grad_in, grad_out)
    grad_tokens = pick_rows(inward(back_rows[:, None])[:, 0])
    ffn_float = ffn_rows.astype(jnp.float32)
    expert_out = (gate_values[:, None] * ffn_float).astype(jnp.bfloat16)
    grad_gates = jnp.sum(cotangent.astype(jnp.float32) * ffn_float, axis=1)
    return (expert_out, grad_tokens, grad_gates, grad_in, grad_out)


def solution(mesh):
    placed = (
        P(("row", "col"), None),
        P(("row", "col"), None),
        P(("row", "col")),
        P(("row", "col"), None, None),
        P(("row", "col"), None, None),
        P(("row", "col"), None),
    )
    return jax.shard_map(
        body,
        mesh=mesh,
        in_specs=placed,
        out_specs=(
            P(("row", "col"), None),
            P(("row", "col"), None),
            P(("row", "col")),
            P(("row", "col"), None, None),
            P(("row", "col"), None, None),
        ),
        check_vma=False,
    )
```

profile of v0, /device:TPU:1, one launch (start us, length us, event | category | flops | bytes accessed | tf_op | source)
XLA Modules:
  0.0 143.7 jit_solution(3776427931755510599)
XLA Ops:
  3.4 3.5 %scatter_custom_fusion = bf16[640,768]{1,0:T(8,128)(2,1)S(1)} fusion(s32[512]{0:T(512)S(1)} %bitcast.146, bf16[512,768]{1,0:T(8,128)(2,1)} %param.8, bf16[]{:T(256)} %constant.19.clone.1), kind=kCustom, calls=%fused_computation.58 | custom fusion | bytes 983552 | tf_op jit(solution)/shard_map/scatter | solution.py:26
  7.0 1.3 broadcast_in_dim_reshape.6
  8.3 11.5 %all-to-all-start = ((bf16[128,1,1,5,768]{4,3,2,1,0:T(8,128)(2,1)}), bf16[128,1,1,5,768]{4,3,2,1,0:T(8,128)(2,1)S(1)}, u32[]{:S(2)}, u32[]{:S(2)}) async-start(bf16[128,1,1,5,768]{4,3,2,1,0:T(8,128)(2,1)} %bitcast.7), calls=%async_computation | async-start | bytes 3145728 | tf_op jit(solution)/shard_map/all_to_all | solution.py:35
  19.8 3.1 %scatter_custom_fusion.1 = bf16[640,768]{1,0:T(8,128)(2,1)S(1)} fusion(s32[512]{0:T(512)S(1)} %bitcast.147, bf16[512,768]{1,0:T(8,128)(2,1)S(1)} %copy-done, f32[512]{0:T(512)S(1)} %copy-done.5, bf16[]{:T(256)} %constant.19.clone.1), kind=kCustom, calls=%fused_computation.51 | custom fusion | flops 1179648 | bytes 1771522 | tf_op jit(solution)/shard_map/scatter | solution.py:26
  22.9 1.3 broadcast_in_dim_reshape.7
  24.3 19.7 %all-to-all-done = bf16[128,1,1,5,768]{4,3,2,1,0:T(8,128)(2,1)S(1)} async-done(((bf16[128,1,1,5,768]{4,3,2,1,0:T(8,128)(2,1)}), bf16[128,1,1,5,768]{4,3,2,1,0:T(8,128)(2,1)S(1)}, u32[]{:S(2)}, u32[]{:S(2)}) %all-to-all-start) | async-done | bytes 983072 | tf_op jit(solution)/shard_map/all_to_all | solution.py:35
  44.0 5.8 %all-to-all-start.2 = ((bf16[128,1,1,5,768]{4,3,2,1,0:T(8,128)(2,1)}), bf16[128,1,1,5,768]{4,3,2,1,0:T(8,128)(2,1)}, u32[]{:S(2)}, u32[]{:S(2)}) async-start(bf16[128,1,1,5,768]{4,3,2,1,0:T(8,128)(2,1)} %bitcast.23), calls=%async_computation.2 | async-start | bytes 3145728 | tf_op jit(solution)/shard_map/all_to_all | solution.py:35
  49.8 5.1 %fusion.17 = f32[128,5,3072]{2,0,1:T(8,128)S(1)} fusion(bf16[1,768,3072]{2,1,0:T(8,128)(2,1)} %param.11, bf16[128,1,1,5,768]{4,3,2,1,0:T(8,128)(2,1)S(1)} %all-to-all-done), kind=kOutput, calls=%fused_computation.28 | convolution fusion | flops 3019898880 | bytes 13565952 | tf_op jit(solution)/shard_map/sjcd,jdf->sjcf/dot_general | solution.py:43
  54.9 9.8 %fusion.40 = bf16[128,1,1,5,768]{4,0,3,2,1:T(8,128)(2,1)S(1)} fusion(bf16[1,3072,768]{2,1,0:T(8,128)(2,1)} %param.12, f32[128,5,3072]{2,0,1:T(8,128)S(1)} %fusion.17), kind=kOutput, calls=%fused_computation.44 | convolution fusion | flops 3038085120 | bytes 13565952 | tf_op jit(solution)/shard_map/sjcf,jfd->sjcd/dot_general | solution.py:45
  64.7 1.7 %copy.26 = bf16[128,1,1,5,768]{4,3,2,1,0:T(8,128)(2,1)} copy(bf16[128,1,1,5,768]{4,0,3,2,1:T(8,128)(2,1)S(1)} %fusion.40) | data formatting | bytes 1966080 | tf_op jit(solution)/shard_map/broadcast_in_dim | solution.py:49
  66.4 7.3 %all-to-all-done.2 = bf16[128,1,1,5,768]{4,3,2,1,0:T(8,128)(2,1)} async-done(((bf16[128,1,1,5,768]{4,3,2,1,0:T(8,128)(2,1)}), bf16[128,1,1,5,768]{4,3,2,1,0:T(8,128)(2,1)}, u32[]{:S(2)}, u32[]{:S(2)}) %all-to-all-start.2) | async-done | bytes 983072 | tf_op jit(solution)/shard_map/all_to_all | solution.py:35
  73.8 4.8 %all-to-all-start.1 = ((bf16[128,1,1,5,768]{4,3,2,1,0:T(8,128)(2,1)}), bf16[128,1,1,5,768]{4,3,2,1,0:T(8,128)(2,1)S(1)}, u32[]{:S(2)}, u32[]{:S(2)}) async-start(bf16[128,1,1,5,768]{4,3,2,1,0:T(8,128)(2,1)} %copy.26), calls=%async_computation.1 | async-start | bytes 3145728 | tf_op jit(solution)/shard_map/all_to_all | solution.py:39
  78.6 10.6 %fusion.6 = bf16[128,1,5,3072]{3,0,2,1:T(8,128)(2,1)S(1)} fusion(f32[128,5,3072]{2,0,1:T(8,128)} %copy-done.6, bf16[1,3072,768]{2,1,0:T(8,128)(2,1)} %param.12, bf16[128,1,1,5,768]{4,3,2,1,0:T(8,128)(2,1)} %all-to-all-done.2), kind=kOutput, calls=%fused_computation.14 | convolution fusion | flops 3059220480 | bytes 17498112 | tf_op jit(solution)/shard_map/sjcd,jfd->sjcf/dot_general | solution.py:51
  89.2 5.8 %fusion.45 = bf16[128,1,1,5,768]{4,0,3,2,1:T(8,128)(2,1)S(1)} fusion(bf16[1,768,3072]{2,1,0:T(8,128)(2,1)} %param.11, bf16[128,1,5,3072]{3,0,2,1:T(8,128)(2,1)S(1)} %fusion.6), kind=kOutput, calls=%fused_computation.45 | convolution fusion | flops 3020390400 | bytes 9633792 | tf_op jit(solution)/shard_map/sjcf,jdf->sjcd/dot_general | solution.py:62
  95.0 1.7 %copy.29 = bf16[128,1,1,5,768]{4,3,2,1,0:T(8,128)(2,1)} copy(bf16[128,1,1,5,768]{4,0,3,2,1:T(8,128)(2,1)S(1)} %fusion.45) | data formatting | bytes 1966080 | tf_op jit(solution)/shard_map/broadcast_in_dim | solution.py:66
  96.7 5.5 %fusion.19 = bf16[1,768,3072]{2,1,0:T(8,128)(2,1)} fusion(bf16[128,1,5,3072]{3,0,2,1:T(8,128)(2,1)S(1)} %fusion.6, bf16[128,5,768]{2,1,0:T(8,128)(2,1)S(1)} %bitcast.138), kind=kOutput, calls=%fused_computation.30 | convolution fusion | flops 3022258176 | bytes 9633792 | tf_op jit(solution)/shard_map/sjcd,sjcf->jdf/dot_general | solution.py:59
  102.8 9.8 %all-to-all-start.3 = ((bf16[128,1,1,5,768]{4,3,2,1,0:T(8,128)(2,1)}), bf16[128,1,1,5,768]{4,3,2,1,0:T(8,128)(2,1)}, u32[]{:S(2)}, u32[]{:S(2)}) async-start(bf16[128,1,1,5,768]{4,3,2,1,0:T(8,128)(2,1)} %copy.29), calls=%async_computation.3 | async-start | bytes 3145728 | tf_op jit(solution)/shard_map/all_to_all | solution.py:39
  112.6 11.0 %fusion.20 = bf16[1,3072,768]{2,1,0:T(8,128)(2,1)} fusion(f32[128,5,3072]{2,0,1:T(8,128)} %copy-done.6, bf16[128,1,1,5,768]{4,3,2,1,0:T(8,128)(2,1)} %all-to-all-done.2), kind=kOutput, calls=%fused_computation.31 | convolution fusion | flops 3039952896 | bytes 13565952 | tf_op jit(solution)/shard_map/sjcf,sjcd->jfd/dot_general | solution.py:56
  124.0 2.7 %gather_fusion = bf16[512,768]{1,0:T(8,128)(2,1)} fusion(bf16[640,768]{1,0:T(8,128)(2,1)S(1)} %reshape_squeeze.6, s32[1024]{0:T(1024)S(1)} %pad_clamp_fusion), kind=kCustom, calls=%fused_computation.clone | custom fusion | bytes 1574912 | tf_op jit(solution)/shard_map/jit(_take)/gather | solution.py:32
  126.7 9.7 %all-to-all-done.3 = bf16[128,1,1,5,768]{4,3,2,1,0:T(8,128)(2,1)} async-done(((bf16[128,1,1,5,768]{4,3,2,1,0:T(8,128)(2,1)}), bf16[128,1,1,5,768]{4,3,2,1,0:T(8,128)(2,1)}, u32[]{:S(2)}, u32[]{:S(2)}) %all-to-all-start.3) | async-done | bytes 983072 | tf_op jit(solution)/shard_map/all_to_all | solution.py:39
  136.4 2.3 %reshape_squeeze.7 = bf16[640,768]{1,0:T(8,128)(2,1)S(1)} reshape(bf16[128,1,1,5,768]{4,3,2,1,0:T(8,128)(2,1)} %all-to-all-done.3) | data formatting | bytes 1966080 | tf_op jit(solution)/shard_map/reshape;squeeze | solution.py:31
  138.7 2.0 %gather_fusion.1 = bf16[512,768]{1,0:T(8,128)(2,1)S(1)} fusion(bf16[640,768]{1,0:T(8,128)(2,1)S(1)} %reshape_squeeze.7, s32[1024]{0:T(1024)S(1)} %pad_clamp_fusion), kind=kCustom, calls=%fused_computation.1.clone | custom fusion | bytes 1574912 | tf_op jit(solution)/shard_map/jit(_take)/gather | solution.py:32
  140.8 1.9 %fusion.29 = (f32[512]{0:T(512)}, bf16[512,768]{1,0:T(8,128)(2,1)}) fusion(bf16[512,768]{1,0:T(8,128)(2,1)S(1)} %copy-done, bf16[512,768]{1,0:T(8,128)(2,1)S(1)} %copy-done.1, pred[512]{0:T(512)(128)(4,1)S(1)} %get-tuple-element.6, f32[512]{0:T(512)S(1)} %copy-done.5), kind=kLoop, calls=%fused_computation.41 | loop fusion | flops 2752000 | bytes 2363904 | tf_op jit(solution)/shard_map/reduce_sum | solution.py:69
  142.7 1.0 broadcast_select_fusion
  (28 shorter events, 3.8 us)
Async XLA Ops:
  0.6 23.6 %copy-start.4 = (s32[512,1]{0,1:T(1,128)S(1)}, s32[512,1]{0,1:T(1,128)}, u32[]{:S(2)}) copy-start(s32[512,1]{0,1:T(1,128)} %param.9) | copy-start | bytes 6148
  0.6 19.2 %copy-start = (bf16[512,768]{1,0:T(8,128)(2,1)S(1)}, bf16[512,768]{1,0:T(8,128)(2,1)}, u32[]{:S(2)}) copy-start(bf16[512,768]{1,0:T(8,128)(2,1)} %param.13) | copy-start | bytes 2359300
  0.7 19.2 %copy-start.5 = (f32[512]{0:T(512)S(1)}, f32[512]{0:T(512)}, u32[]{:S(2)}) copy-start(f32[512]{0:T(512)} %param.10) | copy-start | bytes 6148
  8.3 35.6 %all-to-all-start = ((bf16[128,1,1,5,768]{4,3,2,1,0:T(8,128)(2,1)}), bf16[128,1,1,5,768]{4,3,2,1,0:T(8,128)(2,1)S(1)}, u32[]{:S(2)}, u32[]{:S(2)}) async-start(bf16[128,1,1,5,768]{4,3,2,1,0:T(8,128)(2,1)} %bitcast.7), calls=%async_computation | async-start | bytes 3145728 | tf_op jit(solution)/shard_map/all_to_all | solution.py:35
  44.0 10.9 %copy-start.2 = (bf16[128,1,1,5,768]{4,3,2,1,0:T(8,128)(2,1)}, bf16[128,1,1,5,768]{4,3,2,1,0:T(8,128)(2,1)S(1)}, u32[]{:S(2)}) copy-start(bf16[128,1,1,5,768]{4,3,2,1,0:T(8,128)(2,1)S(1)} %all-to-all-done) | copy-start | bytes 2949124
  44.0 29.8 %all-to-all-start.2 = ((bf16[128,1,1,5,768]{4,3,2,1,0:T(8,128)(2,1)}), bf16[128,1,1,5,768]{4,3,2,1,0:T(8,128)(2,1)}, u32[]{:S(2)}, u32[]{:S(2)}) async-start(bf16[128,1,1,5,768]{4,3,2,1,0:T(8,128)(2,1)} %bitcast.23), calls=%async_computation.2 | async-start | bytes 3145728 | tf_op jit(solution)/shard_map/all_to_all | solution.py:35
  54.9 9.8 %copy-start.6 = (f32[128,5,3072]{2,0,1:T(8,128)}, f32[128,5,3072]{2,0,1:T(8,128)S(1)}, u32[]{:S(2)}) copy-start(f32[128,5,3072]{2,0,1:T(8,128)S(1)} %fusion.17) | copy-start | bytes 23592964
  73.8 29.1 %all-to-all-start.1 = ((bf16[128,1,1,5,768]{4,3,2,1,0:T(8,128)(2,1)}), bf16[128,1,1,5,768]{4,3,2,1,0:T(8,128)(2,1)S(1)}, u32[]{:S(2)}, u32[]{:S(2)}) async-start(bf16[128,1,1,5,768]{4,3,2,1,0:T(8,128)(2,1)} %copy.26), calls=%async_computation.1 | async-start | bytes 3145728 | tf_op jit(solution)/shard_map/all_to_all | solution.py:39
  89.2 7.5 %copy-start.3 = (bf16[128,1,1,5,768]{4,3,2,1,0:T(8,128)(2,1)S(1)}, bf16[128,1,1,5,768]{4,3,2,1,0:T(8,128)(2,1)}, u32[]{:S(2)}) copy-start(bf16[128,1,1,5,768]{4,3,2,1,0:T(8,128)(2,1)} %copy-done.2) | copy-start | bytes 2949124
  102.8 33.6 %all-to-all-start.3 = ((bf16[128,1,1,5,768]{4,3,2,1,0:T(8,128)(2,1)}), bf16[128,1,1,5,768]{4,3,2,1,0:T(8,128)(2,1)}, u32[]{:S(2)}, u32[]{:S(2)}) async-start(bf16[128,1,1,5,768]{4,3,2,1,0:T(8,128)(2,1)} %copy.29), calls=%async_computation.3 | async-start | bytes 3145728 | tf_op jit(solution)/shard_map/all_to_all | solution.py:39
  126.7 14.1 %copy-start.1 = (bf16[512,768]{1,0:T(8,128)(2,1)S(1)}, bf16[512,768]{1,0:T(8,128)(2,1)}, u32[]{:S(2)}) copy-start(bf16[512,768]{1,0:T(8,128)(2,1)} %gather_fusion) | copy-start | bytes 2359300
where the time goes:
time: 144 us
  matrix products  47.8 us (33%)
  waiting for transfers between devices  37.3 us (26%)
  starting transfers between devices  31.9 us (22%)
  local copies, waits for them, and re-layouts  18 us (12%)
  other arithmetic  7.9 us (5%)
    all_to_all x2, waiting for transfers between devices, outward(): lax.all_to_all(stacked, ('row', 'col'), split_axis=0, concat_axis=0, tile...  27 us
    all_to_all x2, starting transfers between devices, outward(): lax.all_to_all(stacked, ('row', 'col'), split_axis=0, concat_axis=0, tile...  17.3 us
    all_to_all x2, starting transfers between devices, inward(): lax.all_to_all(stacked, ('row', 'col'), split_axis=0, concat_axis=0, tile...  14.6 us
    dot_general x1, matrix products, body(): jnp.einsum('sjcf,sjcd->jfd', act_rows, sent_cot, preferred_element_type=j...  11 us
    dot_general x1, matrix products, body(): jnp.einsum('sjcd,jfd->sjcf', sent_cot, weight_out, preferred_element_type...  10.6 us
    all_to_all x2, waiting for transfers between devices, inward(): lax.all_to_all(stacked, ('row', 'col'), split_axis=0, concat_axis=0, tile...  10.3 us
    dot_general x1, matrix products, body(): jnp.einsum('sjcf,jfd->sjcd', act_rows, weight_out, preferred_element_type...  9.8 us
    dot_general x1, matrix products, body(): jnp.einsum('sjcf,jdf->sjcd', grad_pre, weight_in, preferred_element_type=...  5.78 us
  transfers between devices with their start and end apart: 4, of which 4 were waited for; matrix products, arithmetic and copies ran while one was open for 41% of the time, Pallas kernels for 0%

commit v1 on v0

v1 whole, which is shorter than its diff:
```python
import jax
import jax.numpy as jnp
from jax import lax
from jax.experimental import pallas as pl
from jax.experimental.pallas import tpu as pltpu
from jax.sharding import PartitionSpec as P

BF16 = jnp.bfloat16
F32 = jnp.float32
AXES = ("row", "col")
ROOT = 0.7978845608028654
CUBE = 0.044715 * ROOT
FF_CHUNK = 512


def as_column(row):
    size = row.shape[1]
    return jnp.broadcast_to(row, (128, size)).T[:, :1]


def slot_code_row(ids_row, capacity, experts):
    size = ids_row.shape[1]
    ids_col = as_column(ids_row)
    earlier = lax.broadcasted_iota(jnp.int32, (size, size), 0)
    later = lax.broadcasted_iota(jnp.int32, (size, size), 1)
    same = (ids_col == ids_row) & (earlier < later)
    rank = jnp.sum(same.astype(jnp.int32), axis=0, keepdims=True)
    return jnp.where(rank < capacity, rank * experts + ids_row, -1)


def dispatch_kernel(capacity, experts, ids_ref, gate_ref, tokens_ref, cot_ref, out_ref):
    width = tokens_ref.shape[1]
    code = slot_code_row(ids_ref[...], capacity, experts)
    gate = as_column(gate_ref[...])
    scaled = (gate * cot_ref[...].astype(F32)).astype(BF16)
    tokens = tokens_ref[...]
    row = lax.broadcasted_iota(jnp.int32, (2 * experts, 1), 0)
    for k in range(capacity):
        slot = k * experts + (row >> 1)
        pick_tok = (code == jnp.where((row & 1) == 0, slot, -2)).astype(F32).astype(BF16)
        pick_cot = (code == jnp.where((row & 1) == 1, slot, -2)).astype(F32).astype(BF16)
        rows = jnp.dot(pick_tok, tokens, preferred_element_type=F32)
        rows += jnp.dot(pick_cot, scaled, preferred_element_type=F32)
        out_ref[:, :, k * width : (k + 1) * width] = rows.astype(BF16).reshape(experts, 2, width)


def column_kernel(capacity, experts, ids_ref, gate_ref, code_ref, gate_col_ref):
    code_ref[...] = as_column(slot_code_row(ids_ref[...], capacity, experts))
    gate_col_ref[...] = as_column(gate_ref[...])


def nt_dot(a, b):
    return lax.dot_general(a, b, (((1,), (1,)), ((), ())), preferred_element_type=F32)


def tn_dot(a, b):
    return lax.dot_general(a, b, (((0,), (0,)), ((), ())), preferred_element_type=F32)


def expert_kernel(
    capacity, sent_ref, w_in_ref, w_out_ref, back_ref, act_ref, pre_ref, rows_ref, cots_ref
):
    groups = sent_ref.shape[0]
    width, hidden = w_in_ref.shape
    even = lax.broadcasted_iota(jnp.int32, (groups, 2 * groups), 1)
    first = 2 * lax.broadcasted_iota(jnp.int32, (groups, 2 * groups), 0)
    take_tok = (even == first).astype(F32).astype(BF16)
    take_cot = (even == first + 1).astype(F32).astype(BF16)
    for k in range(capacity):
        both = sent_ref[:, :, k * width : (k + 1) * width].reshape(2 * groups, width)
        here = slice(k * groups, (k + 1) * groups)
        rows_ref[here, :] = jnp.dot(take_tok, both, preferred_element_type=F32).astype(BF16)
        cots_ref[here, :] = jnp.dot(take_cot, both, preferred_element_type=F32).astype(BF16)
    for c in range(hidden // FF_CHUNK):
        here = slice(c * FF_CHUNK, (c + 1) * FF_CHUNK)
        v = jnp.dot(rows_ref[...], w_in_ref[:, here], preferred_element_type=F32)
        grad_act = nt_dot(cots_ref[...], w_out_ref[here, :])
        square = v * v
        t = jnp.tanh(v * (ROOT + CUBE * square))
        half = 0.5 * v
        act_ref[:, here] = (half + half * t).astype(BF16)
        slope = (0.5 + 0.5 * t) + (half * (ROOT + 3.0 * CUBE * square)) * (1.0 - t * t)
        pre_ref[:, here] = (grad_act * slope).astype(BF16)
    row = lax.broadcasted_iota(jnp.int32, (2 * groups, groups), 0)
    second = 2 * lax.broadcasted_iota(jnp.int32, (2 * groups, groups), 1)
    put_out = (row == second).astype(F32).astype(BF16)
    put_back = (row == second + 1).astype(F32).astype(BF16)
    out_rows = jnp.dot(act_ref[...], w_out_ref[...], preferred_element_type=F32).astype(BF16)
    back_rows = nt_dot(pre_ref[...], w_in_ref[...]).astype(BF16)
    for k in range(capacity):
        here = slice(k * groups, (k + 1) * groups)
        both = jnp.dot(put_out, out_rows[here, :], preferred_element_type=F32)
        both += jnp.dot(put_back, back_rows[here, :], preferred_element_type=F32)
        back_ref[:, :, k * width : (k + 1) * width] = both.astype(BF16).reshape(groups, 2, width)


def weight_kernel(rows_ref, cots_ref, act_ref, pre_ref, grad_in_ref, grad_out_ref):
    grad_in_ref[...] = tn_dot(rows_ref[...], pre_ref[...]).astype(BF16)
    grad_out_ref[...] = tn_dot(act_ref[...], cots_ref[...]).astype(BF16)


def combine_kernel(
    capacity, experts, got_ref, code_ref, gate_ref, cot_ref, out_ref, grad_tok_ref, grad_gate_ref
):
    tok_dev, width = cot_ref.shape
    code = code_ref[...]
    column = lax.broadcasted_iota(jnp.int32, (1, 2 * experts), 1)
    ffn = jnp.zeros((tok_dev, width), F32)
    back = jnp.zeros((tok_dev, width), F32)
    for k in range(capacity):
        both = got_ref[:, :, k * width : (k + 1) * width].reshape(2 * experts, width)
        slot = k * experts + (column >> 1)
        pick_out = (code == jnp.where((column & 1) == 0, slot, -2)).astype(F32).astype(BF16)
        pick_back = (code == jnp.where((column & 1) == 1, slot, -2)).astype(F32).astype(BF16)
        ffn += jnp.dot(pick_out, both, preferred_element_type=F32)
        back += jnp.dot(pick_back, both, preferred_element_type=F32)
    grad_tok_ref[...] = back.astype(BF16)
    out_ref[...] = (gate_ref[...] * ffn).astype(BF16)
    grad_gate = jnp.sum(cot_ref[...].astype(F32) * ffn, axis=1, keepdims=True)
    grad_gate_ref[...] = jnp.broadcast_to(grad_gate, (tok_dev, 128)).T[:1, :]


def params(mib):
    return pltpu.CompilerParams(vmem_limit_bytes=mib << 20)


def body(tokens, expert_ids, gate_values, weight_in, weight_out, cotangent):
    tok_dev, width = tokens.shape
    exp_dev, _, hidden = weight_in.shape
    experts = exp_dev * lax.axis_size("row") * lax.axis_size("col")
    groups = experts
    capacity = max(2, (5 * tok_dev + 4 * experts - 1) // (4 * experts))
    slots = groups * capacity
    ids_row = expert_ids.reshape(1, tok_dev)
    gate_row = gate_values.reshape(1, tok_dev)
    w_in = weight_in.reshape(width, hidden)
    w_out = weight_out.reshape(hidden, width)
    mxu = 2 * slots * width * hidden

    def shape(dims, kind=BF16):
        return jax.ShapeDtypeStruct(dims, kind)

    def exchange(x):
        return lax.all_to_all(x, AXES, split_axis=0, concat_axis=0, tiled=True)

    packed = shape((groups, 2, capacity * width))
    sent = pl.pallas_call(
        lambda *refs: dispatch_kernel(capacity, experts, *refs),
        out_shape=packed,
        compiler_params=params(24),
    )(ids_row, gate_row, tokens, cotangent)
    code, gate_col = pl.pallas_call(
        lambda *refs: column_kernel(capacity, experts, *refs),
        out_shape=(shape((tok_dev, 1), jnp.int32), shape((tok_dev, 1), F32)),
        compiler_params=params(16),
    )(ids_row, gate_row)
    sent = exchange(sent)
    back, act, pre, rows, cots = pl.pallas_call(
        lambda *refs: expert_kernel(capacity, *refs),
        out_shape=(
            packed,
            shape((slots, hidden)),
            shape((slots, hidden)),
            shape((slots, width)),
            shape((slots, width)),
        ),
        compiler_params=params(48),
        cost_estimate=pl.CostEstimate(
            flops=4 * mxu, bytes_accessed=20 << 20, transcendentals=slots * hidden
        ),
    )(sent, w_in, w_out)
    back = exchange(back)
    whole = pl.BlockSpec((slots, width), lambda j: (0, 0))
    part = pl.BlockSpec((slots, FF_CHUNK), lambda j: (0, j))
    grad_in, grad_out = pl.pallas_call(
        weight_kernel,
        grid=(hidden // FF_CHUNK,),
        in_specs=[whole, whole, part, part],
        out_specs=[
            pl.BlockSpec((width, FF_CHUNK), lambda j: (0, j)),
            pl.BlockSpec((FF_CHUNK, width), lambda j: (j, 0)),
        ],
        out_shape=(shape((width, hidden)), shape((hidden, width))),
        compiler_params=params(24),
        cost_estimate=pl.CostEstimate(
            flops=2 * mxu, bytes_accessed=20 << 20, transcendentals=0
        ),
    )(rows, cots, act, pre)
    expert_out, grad_tokens, grad_gates = pl.pallas_call(
        lambda *refs: combine_kernel(capacity, experts, *refs),
        out_shape=(shape((tok_dev, width)), shape((tok_dev, width)), shape((1, tok_dev), F32)),
        compiler_params=params(24),
    )(back, code, gate_col, cotangent)
    return (
        expert_out,
        grad_tokens,
        grad_gates.reshape(tok_dev),
        grad_in.reshape(weight_in.shape),
        grad_out.reshape(weight_out.shape),
    )


def solution(mesh):
    placed = (
        P(AXES, None),
        P(AXES, None),
        P(AXES),
        P(AXES, None, None),
        P(AXES, None, None),
        P(AXES, None),
    )
    return jax.shard_map(
        body,
        mesh=mesh,
        in_specs=placed,
        out_specs=(
            P(AXES, None),
            P(AXES, None),
            P(AXES),
            P(AXES, None, None),
            P(AXES, None, None),
        ),
        check_vma=False,
    )
```

time: 144 us -> 106 us (0.74)
  matrix products: 47.8 us -> 0 us
  blocking collectives: 0 us -> 39.5 us
  Pallas kernels: 0 us -> 35.7 us
  starting transfers between devices: 31.9 us -> 4.85 us
  waiting for transfers between devices: 37.3 us -> 11.1 us
  other arithmetic: 7.9 us -> 0 us
  local copies, waits for them, and re-layouts: 18 us -> 13.5 us
    dot_general x6 -> x0, matrix products: 47.8 us -> none  [the longest x1 11 us: body(): jnp.einsum('sjcf,sjcd->jfd', act_rows, sent_cot, preferred_element_type=j...]
    all_to_all x0 -> x1, blocking collectives: none -> 39.5 us  [exchange(): return lax.all_to_all(x, AXES, split_axis=0, concat_axis=0, tiled=True)]
    pallas_call x0 -> x5, Pallas kernels: none -> 35.7 us  [the longest x1 19.1 us: body(): pl.pallas_call(lambda *refs: expert_kernel(capacity, *refs), out_shape=(p...]
    all_to_all x4 -> x1, starting transfers between devices: 31.9 us -> 4.85 us  [exchange(): return lax.all_to_all(x, AXES, split_axis=0, concat_axis=0, tiled=True)]
    all_to_all x4 -> x1, waiting for transfers between devices: 37.3 us -> 11.1 us  [exchange(): return lax.all_to_all(x, AXES, split_axis=0, concat_axis=0, tiled=True)]
    unnamed x15 -> x28, local copies, waits for them, and re-layouts: 0.04 us -> 13.5 us
    another operation x7 -> x0, local copies, waits for them, and re-layouts: 5.45 us -> none  [the longest x2 2.73 us: pick_rows(): flat_rows = source.reshape(experts * capacity, model_width)]
    gather x2 -> x0, local copies, waits for them, and re-layouts: 4.74 us -> none  [pick_rows(): return jnp.take(flat_rows, position, axis=0, mode='fill', fill_value=0)]
  transfers between devices with their start and end apart: 4 -> 1, of which waited for: 4 -> 1; matrix products, arithmetic and copies ran while one was open for 41% -> 0% of each run, Pallas kernels for 0% -> 10%
where the time goes in v1:
time: 106 us; the launch traced here: 105 us
  blocking collectives  39.5 us (37%)
  Pallas kernels  35.7 us (34%)
  local copies, waits for them, and re-layouts  13.5 us (13%)
  waiting for transfers between devices  11.1 us (10%)
  starting transfers between devices  4.85 us (5%)
    all_to_all x1, blocking collectives, exchange(): return lax.all_to_all(x, AXES, split_axis=0, concat_axis=0, tiled=True)  39.5 us
    pallas_call x1, Pallas kernels, body(): pl.pallas_call(lambda *refs: expert_kernel(capacity, *refs), out_shape=(p...  19.1 us
    unnamed x28, local copies, waits for them, and re-layouts  13.5 us
    all_to_all x1, waiting for transfers between devices, exchange(): return lax.all_to_all(x, AXES, split_axis=0, concat_axis=0, tiled=True)  11.1 us
    pallas_call x1, Pallas kernels, body(): pl.pallas_call(weight_kernel, grid=(hidden // FF_CHUNK,), in_specs=[whole...  10.1 us
    all_to_all x1, starting transfers between devices, exchange(): return lax.all_to_all(x, AXES, split_axis=0, concat_axis=0, tiled=True)  4.85 us
    pallas_call x1, Pallas kernels, body(): pl.pallas_call(lambda *refs: combine_kernel(capacity, experts, *refs), ou...  3.39 us
    pallas_call x1, Pallas kernels, body(): pl.pallas_call(lambda *refs: dispatch_kernel(capacity, experts, *refs), o...  2.66 us
  transfers between devices with their start and end apart: 1, of which 1 were waited for; matrix products, arithmetic and copies ran while one was open for 0% of the time, Pallas kernels for 10%

profile of v1, /device:TPU:1, one launch (start us, length us, event | category | flops | bytes accessed | tf_op | source)
XLA Modules:
  0.0 105.3 jit_solution(8544465957245350187)
XLA Ops:
  0.6 0.0 copy-start
  0.6 1.1 %copy-done = bf16[512,768]{1,0:T(8,128)(2,1)S(1)} copy-done((bf16[512,768]{1,0:T(8,128)(2,1)S(1)}, bf16[512,768]{1,0:T(8,128)(2,1)}, u32[]{:S(2)}) %copy-start) | copy-done | bytes 786456
  1.8 1.1 %copy-done.3 = bf16[512,768]{1,0:T(8,128)(2,1)S(1)} copy-done((bf16[512,768]{1,0:T(8,128)(2,1)S(1)}, bf16[512,768]{1,0:T(8,128)(2,1)}, u32[]{:S(2)}) %copy-start.3) | copy-done | bytes 786456
  2.9 0.7 copy-done.4
  3.6 0.7 copy-done.6
  4.3 2.7 %shard_map.101 = bf16[128,2,3840]{2,1,0:T(2,128)(2,1)S(1)} custom-call(s32[1,512]{1,0:T(1,128)S(1)} %bitcast.7, f32[1,512]{1,0:T(1,128)S(1)} %bitcast.9, bf16[512,768]{1,0:T(8,128)(2,1)S(1)} %copy-done.3, bf16[512,768]{1,0:T(8,128)(2,1)S(1)} %copy-done), custom_call_target="tpu_custom_call" | custom-call | tf_op jit(solution)/shard_map/pallas_call | solution.py:147
  6.9 39.5 %all_to_all.10.refs_0_ = bf16[128,2,3840]{2,1,0:T(2,128)(2,1)S(1)} all-to-all(bf16[128,2,3840]{2,1,0:T(2,128)(2,1)S(1)} %shard_map.101), channel_id=1, replica_groups=mesh['row'=8,'col'=16] {'row','col'}, dimensions={0} | all-to-all | bytes 3932160 | tf_op jit(solution)/shard_map/all_to_all | solution.py:144
  46.4 19.1 %shard_map.102 = (bf16[128,2,3840]{2,1,0:T(2,128)(2,1)S(1)}, bf16[640,3072]{1,0:T(8,128)(2,1)}, bf16[640,3072]{1,0:T(8,128)(2,1)}, bf16[640,768]{1,0:T(8,128)(2,1)S(1)}, bf16[640,768]{1,0:T(8,128)(2,1)S(1)}) custom-call(bf16[128,2,3840]{2,1,0:T(2,128)(2,1)S(1)} %all_to_all.10.refs_0_, bf16[768,3072]{1,0:T(8,128)(2,1)} %bitcast.11, bf16[3072,768]{1,0:T(8,128)(2,1)} %bitcast.12), custom_call_target="tpu_custom_call" | custom-call | flops 12079595520 | bytes 20971520 | tf_op jit(solution)/shard_map/pallas_call | solution.py:158
  65.5 0.0 copy-start.2
  65.5 1.3 %copy-done.2 = bf16[128,2,3840]{2,1,0:T(2,128)(2,1)} copy-done((bf16[128,2,3840]{2,1,0:T(2,128)(2,1)}, bf16[128,2,3840]{2,1,0:T(2,128)(2,1)S(1)}, u32[]{:S(2)}) %copy-start.2) | copy-done | bytes 1966104
  66.8 1.0 copy-done.10
  67.8 1.0 copy-done.12
  68.8 4.8 %all-to-all-start.1 = ((bf16[128,2,3840]{2,1,0:T(2,128)(2,1)}), bf16[128,2,3840]{2,1,0:T(2,128)(2,1)S(1)}, u32[]{:S(2)}, u32[]{:S(2)}) async-start(bf16[128,2,3840]{2,1,0:T(2,128)(2,1)} %copy-done.2), calls=%async_computation.1 | async-start | bytes 3932160 | tf_op jit(solution)/shard_map/all_to_all | solution.py:144
  73.6 0.0 copy-done.5
  73.6 0.0 copy-done.7
  73.6 0.4 shard_map.103
  74.0 0.0 copy-start.8
  74.1 2.1 %copy-done.8 = bf16[640,3072]{1,0:T(8,128)(2,1)S(1)} copy-done((bf16[640,3072]{1,0:T(8,128)(2,1)S(1)}, bf16[640,3072]{1,0:T(8,128)(2,1)}, u32[]{:S(2)}) %copy-start.8) | copy-done | bytes 3932184
  76.2 2.1 %copy-done.9 = bf16[640,3072]{1,0:T(8,128)(2,1)S(1)} copy-done((bf16[640,3072]{1,0:T(8,128)(2,1)S(1)}, bf16[640,3072]{1,0:T(8,128)(2,1)}, u32[]{:S(2)}) %copy-start.9) | copy-done | bytes 3932184
  78.3 1.2 %copy-done.11 = bf16[640,768]{1,0:T(8,128)(2,1)S(1)} copy-done((bf16[640,768]{1,0:T(8,128)(2,1)S(1)}, bf16[640,768]{1,0:T(8,128)(2,1)}, u32[]{:S(2)}) %copy-start.11) | copy-done | bytes 983064
  79.5 1.2 %copy-done.13 = bf16[640,768]{1,0:T(8,128)(2,1)S(1)} copy-done((bf16[640,768]{1,0:T(8,128)(2,1)S(1)}, bf16[640,768]{1,0:T(8,128)(2,1)}, u32[]{:S(2)}) %copy-start.13) | copy-done | bytes 983064
  80.7 10.1 %shard_map.105 = (bf16[768,3072]{1,0:T(8,128)(2,1)}, bf16[3072,768]{1,0:T(8,128)(2,1)}) custom-call(bf16[640,768]{1,0:T(8,128)(2,1)S(1)} %copy-done.11, bf16[640,768]{1,0:T(8,128)(2,1)S(1)} %copy-done.13, bf16[640,3072]{1,0:T(8,128)(2,1)S(1)} %copy-done.8, bf16[640,3072]{1,0:T(8,128)(2,1)S(1)} %copy-done.9), custom_call_target="tpu_custom_call" | custom-call | flops 6039797760 | bytes 20971520 | tf_op jit(solution)/shard_map/pallas_call | solution.py:175
  90.8 11.1 %all-to-all-done.1.refs_0_ = bf16[128,2,3840]{2,1,0:T(2,128)(2,1)S(1)} async-done(((bf16[128,2,3840]{2,1,0:T(2,128)(2,1)}), bf16[128,2,3840]{2,1,0:T(2,128)(2,1)S(1)}, u32[]{:S(2)}, u32[]{:S(2)}) %all-to-all-start.1) | async-done | bytes 1966112 | tf_op jit(solution)/shard_map/all_to_all | solution.py:144
  101.9 3.4 %shard_map.104 = (bf16[512,768]{1,0:T(8,128)(2,1)}, bf16[512,768]{1,0:T(8,128)(2,1)}, f32[1,512]{1,0:T(1,128)}) custom-call(bf16[128,2,3840]{2,1,0:T(2,128)(2,1)S(1)} %all-to-all-done.1.refs_0_, s32[512,1]{1,0:T(8,128)S(1)} %get-tuple-element.18.refs_1_, f32[512,1]{1,0:T(8,128)S(1)} %get-tuple-element.19.refs_2_, bf16[512,768]{1,0:T(8,128)(2,1)S(1)} %copy-done.1), custom_call_target="tpu_custom_call" | custom-call | tf_op jit(solution)/shard_map/pallas_call | solution.py:189
  (12 shorter events, 0.0 us)
Async XLA Ops:
  0.6 1.1 %copy-start = (bf16[512,768]{1,0:T(8,128)(2,1)S(1)}, bf16[512,768]{1,0:T(8,128)(2,1)}, u32[]{:S(2)}) copy-start(bf16[512,768]{1,0:T(8,128)(2,1)} %refs_3_.3) | copy-start | bytes 2359300
  1.8 1.1 %copy-start.3 = (bf16[512,768]{1,0:T(8,128)(2,1)S(1)}, bf16[512,768]{1,0:T(8,128)(2,1)}, u32[]{:S(2)}) copy-start(bf16[512,768]{1,0:T(8,128)(2,1)} %refs_2_.1) | copy-start | bytes 2359300
  2.9 0.7 copy-start.4
  3.6 0.7 copy-start.6
  65.5 1.3 %copy-start.2 = (bf16[128,2,3840]{2,1,0:T(2,128)(2,1)}, bf16[128,2,3840]{2,1,0:T(2,128)(2,1)S(1)}, u32[]{:S(2)}) copy-start(bf16[128,2,3840]{2,1,0:T(2,128)(2,1)S(1)} %get-tuple-element.17) | copy-start | bytes 5898244
  66.8 1.0 copy-start.10
  67.8 1.0 copy-start.12
  68.7 4.9 %copy-start.5 = (s32[512,1]{0,1:T(1,128)S(1)}, s32[512,1]{0,1:T(1,128)}, u32[]{:S(2)}) copy-start(s32[512,1]{0,1:T(1,128)} %param.7) | copy-start | bytes 6148
  68.7 4.9 %copy-start.7 = (f32[512]{0:T(512)S(1)}, f32[512]{0:T(512)}, u32[]{:S(2)}) copy-start(f32[512]{0:T(512)} %param.8) | copy-start | bytes 6148
  68.8 33.2 %all-to-all-start.1 = ((bf16[128,2,3840]{2,1,0:T(2,128)(2,1)}), bf16[128,2,3840]{2,1,0:T(2,128)(2,1)S(1)}, u32[]{:S(2)}, u32[]{:S(2)}) async-start(bf16[128,2,3840]{2,1,0:T(2,128)(2,1)} %copy-done.2), calls=%async_computation.1 | async-start | bytes 3932160 | tf_op jit(solution)/shard_map/all_to_all | solution.py:144
  74.0 2.1 %copy-start.8 = (bf16[640,3072]{1,0:T(8,128)(2,1)S(1)}, bf16[640,3072]{1,0:T(8,128)(2,1)}, u32[]{:S(2)}) copy-start(bf16[640,3072]{1,0:T(8,128)(2,1)} %get-tuple-element.25.act_ref) | copy-start | bytes 11796484
  76.2 2.1 %copy-start.9 = (bf16[640,3072]{1,0:T(8,128)(2,1)S(1)}, bf16[640,3072]{1,0:T(8,128)(2,1)}, u32[]{:S(2)}) copy-start(bf16[640,3072]{1,0:T(8,128)(2,1)} %get-tuple-element.26.pre_ref) | copy-start | bytes 11796484
  78.3 1.2 %copy-start.11 = (bf16[640,768]{1,0:T(8,128)(2,1)S(1)}, bf16[640,768]{1,0:T(8,128)(2,1)}, u32[]{:S(2)}) copy-start(bf16[640,768]{1,0:T(8,128)(2,1)} %copy-done.10) | copy-start | bytes 2949124
  79.5 1.2 %copy-start.13 = (bf16[640,768]{1,0:T(8,128)(2,1)S(1)}, bf16[640,768]{1,0:T(8,128)(2,1)}, u32[]{:S(2)}) copy-start(bf16[640,768]{1,0:T(8,128)(2,1)} %copy-done.12) | copy-start | bytes 2949124
  80.7 21.3 %copy-start.1 = (bf16[512,768]{1,0:T(8,128)(2,1)S(1)}, bf16[512,768]{1,0:T(8,128)(2,1)}, u32[]{:S(2)}) copy-start(bf16[512,768]{1,0:T(8,128)(2,1)} %refs_3_.3) | copy-start | bytes 2359300

commit v2 on v1

v2 whole, which is shorter than its diff:
```python
import jax
import jax.numpy as jnp
from jax import lax
from jax.experimental import pallas as pl
from jax.experimental.pallas import tpu as pltpu
from jax.sharding import PartitionSpec as P

BF16 = jnp.bfloat16
F32 = jnp.float32
AXES = ("row", "col")
ROOT = 0.7978845608028654
CUBE = 0.044715 * ROOT
FF_CHUNK = 512
EXPERT_CHUNK = 512
EXPERT_MIB = 60
WEIGHT_MIB = 48


def as_column(row):
    size = row.shape[1]
    return jnp.broadcast_to(row, (128, size)).T[:, :1]


def slot_code_row(ids_row, capacity, experts):
    size = ids_row.shape[1]
    ids_col = as_column(ids_row)
    earlier = lax.broadcasted_iota(jnp.int32, (size, size), 0)
    later = lax.broadcasted_iota(jnp.int32, (size, size), 1)
    same = (ids_col == ids_row) & (earlier < later)
    rank = jnp.sum(same.astype(jnp.int32), axis=0, keepdims=True)
    return jnp.where(rank < capacity, rank * experts + ids_row, -1)


def pair_matrix(size):
    row = lax.broadcasted_iota(jnp.int32, (2 * size, 2 * size), 0)
    column = lax.broadcasted_iota(jnp.int32, (2 * size, 2 * size), 1)
    second = (row >= size).astype(jnp.int32)
    return (column == 2 * (row - second * size) + second).astype(F32).astype(BF16)


def unpair_matrix(size):
    row = lax.broadcasted_iota(jnp.int32, (2 * size, 2 * size), 0)
    column = lax.broadcasted_iota(jnp.int32, (2 * size, 2 * size), 1)
    second = (column >= size).astype(jnp.int32)
    return (row == 2 * (column - second * size) + second).astype(F32).astype(BF16)


def join_pairs(capacity, first, second, pairs_ref, pairs_hbm, sems):
    size = pairs_ref.shape[0]
    width = first.shape[1]
    join = unpair_matrix(size)
    copies = []
    for k in range(capacity):
        here = slice(k * size, (k + 1) * size)
        both = jnp.concatenate([first[here, :], second[here, :]], axis=0)
        both = jnp.dot(join, both, preferred_element_type=F32).astype(BF16)
        part = slice(k * width, (k + 1) * width)
        pairs_ref[:, :, part] = both.reshape(size, 2, width)
        copy = pltpu.make_async_copy(
            pairs_ref.at[:, :, part], pairs_hbm.at[:, :, part], sems.at[k]
        )
        copy.start()
        copies.append(copy)
    for copy in copies:
        copy.wait()


def dispatch_kernel(
    capacity,
    experts,
    ids_hbm,
    gate_hbm,
    tokens_hbm,
    cot_hbm,
    out_hbm,
    ids_ref,
    gate_ref,
    tokens_ref,
    cot_ref,
    out_ref,
    in_sems,
    sems,
):
    fetches = [
        pltpu.make_async_copy(source, target, in_sems.at[i])
        for i, (source, target) in enumerate(
            (
                (ids_hbm, ids_ref),
                (gate_hbm, gate_ref),
                (tokens_hbm, tokens_ref),
                (cot_hbm, cot_ref),
            )
        )
    ]
    for fetch in fetches:
        fetch.start()
    fetches[0].wait()
    code = slot_code_row(ids_ref[...], capacity, experts)
    slot = lax.broadcasted_iota(jnp.int32, (experts * capacity, 1), 0)
    pick = (code == slot).astype(F32).astype(BF16)
    for fetch in fetches[1:]:
        fetch.wait()
    gate = as_column(gate_ref[...])
    rows = jnp.dot(pick, tokens_ref[...], preferred_element_type=F32).astype(BF16)
    scaled = (gate * cot_ref[...].astype(F32)).astype(BF16)
    cots = jnp.dot(pick, scaled, preferred_element_type=F32).astype(BF16)
    join_pairs(capacity, rows, cots, out_ref, out_hbm, sems)


def column_kernel(capacity, experts, ids_ref, gate_ref, info_ref):
    code = slot_code_row(ids_ref[...], capacity, experts)
    info_ref[:, 0:1] = as_column(code.astype(F32))
    info_ref[:, 1:2] = as_column(gate_ref[...])


def nt_dot(a, b):
    return lax.dot_general(a, b, (((1,), (1,)), ((), ())), preferred_element_type=F32)


def tn_dot(a, b):
    return lax.dot_general(a, b, (((0,), (0,)), ((), ())), preferred_element_type=F32)


def split_pairs(capacity, pairs_ref, first_ref, second_ref, fetches=None):
    groups = pairs_ref.shape[0]
    width = first_ref.shape[1]
    split = pair_matrix(groups)
    for k in range(capacity):
        if fetches is not None:
            fetches[k].wait()
        both = pairs_ref[:, :, k * width : (k + 1) * width].reshape(2 * groups, width)
        both = jnp.dot(split, both, preferred_element_type=F32).astype(BF16)
        here = slice(k * groups, (k + 1) * groups)
        first_ref[here, :] = both[:groups]
        second_ref[here, :] = both[groups:]


def activate(v, grad_act):
    square = v * v
    t = jnp.tanh(v * (ROOT + CUBE * square))
    half = 0.5 * v
    slope = (0.5 + 0.5 * t) + (half * (ROOT + 3.0 * CUBE * square)) * (1.0 - t * t)
    return (half + half * t).astype(BF16), (grad_act * slope).astype(BF16)


def expert_kernel(
    capacity,
    sent_hbm,
    w_in_hbm,
    w_out_hbm,
    back_hbm,
    sent_ref,
    w_in_ref,
    w_out_ref,
    act_ref,
    pre_ref,
    rows_ref,
    cots_ref,
    sent_sems,
    w_sems,
    sems,
):
    width, hidden = w_in_ref.shape
    parts = [slice(c, c + EXPERT_CHUNK) for c in range(0, hidden, EXPERT_CHUNK)]
    lanes = [slice(k * width, (k + 1) * width) for k in range(capacity)]
    arrivals = [
        pltpu.make_async_copy(sent_hbm.at[:, :, part], sent_ref.at[:, :, part], sent_sems.at[k])
        for k, part in enumerate(lanes)
    ]
    fetches = [
        (
            pltpu.make_async_copy(w_in_hbm.at[:, here], w_in_ref.at[:, here], w_sems.at[0, c]),
            pltpu.make_async_copy(w_out_hbm.at[here, :], w_out_ref.at[here, :], w_sems.at[1, c]),
        )
        for c, here in enumerate(parts)
    ]
    for fetch in arrivals:
        fetch.start()
    for pair in fetches[:1]:
        for fetch in pair:
            fetch.start()
    split_pairs(capacity, sent_ref, rows_ref, cots_ref, arrivals)
    for pair in fetches[1:]:
        for fetch in pair:
            fetch.start()
    for c, here in enumerate(parts):
        for pair in fetches[c : c + 1] if c < 2 else fetches[2:] if c == 2 else []:
            for fetch in pair:
                fetch.wait()
        v = jnp.dot(rows_ref[...], w_in_ref[:, here], preferred_element_type=F32)
        grad_act = nt_dot(cots_ref[...], w_out_ref[here, :])
        act_ref[:, here], pre_ref[:, here] = activate(v, grad_act)
    out_rows = jnp.dot(act_ref[...], w_out_ref[...], preferred_element_type=F32).astype(BF16)
    back_rows = nt_dot(pre_ref[...], w_in_ref[...]).astype(BF16)
    join_pairs(capacity, out_rows, back_rows, sent_ref, back_hbm, sems)


def weight_kernel(
    capacity, sent_ref, w_in_ref, w_out_ref, grad_in_ref, grad_out_ref, rows_ref, cots_ref
):
    @pl.when(pl.program_id(0) == 0)
    def _():
        split_pairs(capacity, sent_ref, rows_ref, cots_ref)

    v = jnp.dot(rows_ref[...], w_in_ref[...], preferred_element_type=F32)
    grad_act = nt_dot(cots_ref[...], w_out_ref[...])
    act, pre = activate(v, grad_act)
    grad_in_ref[...] = tn_dot(rows_ref[...], pre).astype(BF16)
    grad_out_ref[...] = tn_dot(act, cots_ref[...]).astype(BF16)


def combine_kernel(
    capacity, experts, got_ref, info_ref, cot_ref, out_ref, grad_tok_ref, grad_gate_ref
):
    tok_dev, width = cot_ref.shape
    code = info_ref[:, 0:1].astype(jnp.int32)
    column = lax.broadcasted_iota(jnp.int32, (1, 2 * experts), 1)
    ffn = jnp.zeros((tok_dev, width), F32)
    back = jnp.zeros((tok_dev, width), F32)
    for k in range(capacity):
        both = got_ref[:, :, k * width : (k + 1) * width].reshape(2 * experts, width)
        slot = k * experts + (column >> 1)
        pick_out = (code == jnp.where((column & 1) == 0, slot, -2)).astype(F32).astype(BF16)
        pick_back = (code == jnp.where((column & 1) == 1, slot, -2)).astype(F32).astype(BF16)
        ffn += jnp.dot(pick_out, both, preferred_element_type=F32)
        back += jnp.dot(pick_back, both, preferred_element_type=F32)
    grad_tok_ref[...] = back.astype(BF16)
    out_ref[...] = (info_ref[:, 1:2] * ffn).astype(BF16)
    grad_gate = jnp.sum(cot_ref[...].astype(F32) * ffn, axis=1, keepdims=True)
    grad_gate_ref[...] = jnp.broadcast_to(grad_gate, (tok_dev, 128)).T[:1, :]


def params(mib):
    return pltpu.CompilerParams(vmem_limit_bytes=mib << 20)


def body(tokens, expert_ids, gate_values, weight_in, weight_out, cotangent):
    tok_dev, width = tokens.shape
    exp_dev, _, hidden = weight_in.shape
    experts = exp_dev * lax.axis_size("row") * lax.axis_size("col")
    groups = experts
    capacity = max(2, (5 * tok_dev + 4 * experts - 1) // (4 * experts))
    slots = groups * capacity
    ids_row = expert_ids.reshape(1, tok_dev)
    gate_row = gate_values.reshape(1, tok_dev)
    w_in = weight_in.reshape(width, hidden)
    w_out = weight_out.reshape(hidden, width)
    mxu = 2 * slots * width * hidden

    def shape(dims, kind=BF16):
        return jax.ShapeDtypeStruct(dims, kind)

    def exchange(x):
        return lax.all_to_all(x, AXES, split_axis=0, concat_axis=0, tiled=True)

    vmem = pl.BlockSpec(memory_space=pltpu.VMEM)
    hbm = pl.BlockSpec(memory_space=pltpu.HBM)
    packed = shape((groups, 2, capacity * width))
    block = pltpu.VMEM((slots, width), BF16)
    token_block = pltpu.VMEM((tok_dev, width), BF16)
    sent = pl.pallas_call(
        lambda *refs: dispatch_kernel(capacity, experts, *refs),
        in_specs=[hbm] * 4,
        out_specs=hbm,
        out_shape=packed,
        scratch_shapes=[
            pltpu.VMEM(ids_row.shape, jnp.int32),
            pltpu.VMEM(gate_row.shape, F32),
            token_block,
            token_block,
            pltpu.VMEM(packed.shape, BF16),
            pltpu.SemaphoreType.DMA((4,)),
            pltpu.SemaphoreType.DMA((capacity,)),
        ],
        compiler_params=params(62),
    )(ids_row, gate_row, tokens, cotangent)
    info = pl.pallas_call(
        lambda *refs: column_kernel(capacity, experts, *refs),
        out_shape=shape((tok_dev, 2), F32),
        compiler_params=params(16),
    )(ids_row, gate_row)
    sent = exchange(sent)
    back = pl.pallas_call(
        lambda *refs: expert_kernel(capacity, *refs),
        in_specs=[hbm] * 3,
        out_specs=hbm,
        out_shape=packed,
        scratch_shapes=[
            pltpu.VMEM(packed.shape, BF16),
            pltpu.VMEM((width, hidden), BF16),
            pltpu.VMEM((hidden, width), BF16),
            pltpu.VMEM((slots, hidden), BF16),
            pltpu.VMEM((slots, hidden), BF16),
            block,
            block,
            pltpu.SemaphoreType.DMA((capacity,)),
            pltpu.SemaphoreType.DMA((2, hidden // EXPERT_CHUNK)),
            pltpu.SemaphoreType.DMA((capacity,)),
        ],
        compiler_params=params(EXPERT_MIB),
        cost_estimate=pl.CostEstimate(
            flops=4 * mxu, bytes_accessed=13 << 20, transcendentals=slots * hidden
        ),
    )(sent, w_in, w_out)
    back = exchange(back)
    in_part = pl.BlockSpec((width, FF_CHUNK), lambda j: (0, j))
    out_part = pl.BlockSpec((FF_CHUNK, width), lambda j: (j, 0))
    grad_in, grad_out = pl.pallas_call(
        lambda *refs: weight_kernel(capacity, *refs),
        grid=(hidden // FF_CHUNK,),
        in_specs=[vmem, in_part, out_part],
        out_specs=[in_part, out_part],
        out_shape=(shape((width, hidden)), shape((hidden, width))),
        scratch_shapes=[block, block],
        compiler_params=params(WEIGHT_MIB),
        cost_estimate=pl.CostEstimate(
            flops=4 * mxu, bytes_accessed=21 << 20, transcendentals=slots * hidden
        ),
    )(sent, w_in, w_out)
    expert_out, grad_tokens, grad_gates = pl.pallas_call(
        lambda *refs: combine_kernel(capacity, experts, *refs),
        out_shape=(shape((tok_dev, width)), shape((tok_dev, width)), shape((1, tok_dev), F32)),
        compiler_params=params(24),
    )(back, info, cotangent)
    return (
        expert_out,
        grad_tokens,
        grad_gates.reshape(tok_dev),
        grad_in.reshape(weight_in.shape),
        grad_out.reshape(weight_out.shape),
    )


def solution(mesh):
    placed = (
        P(AXES, None),
        P(AXES, None),
        P(AXES),
        P(AXES, None, None),
        P(AXES, None, None),
        P(AXES, None),
    )
    return jax.shard_map(
        body,
        mesh=mesh,
        in_specs=placed,
        out_specs=(
            P(AXES, None),
            P(AXES, None),
            P(AXES),
            P(AXES, None, None),
            P(AXES, None, None),
        ),
        check_vma=False,
    )
```

time: 106 us -> 99.6 us (0.940)
  local copies, waits for them, and re-layouts: 13.5 us -> 1.55 us
  Pallas kernels: 35.7 us -> 45.9 us
  waiting for transfers between devices: 11.1 us -> 6.6 us
    unnamed x28 -> x8, local copies, waits for them, and re-layouts: 13.5 us -> 1.55 us
    pallas_call x3, Pallas kernels: 31.9 us -> 41.9 us  [the longest x1 19.6 us: body(): pl.pallas_call(lambda *refs: weight_kernel(capacity, *refs), grid=(hidden...]
    all_to_all x1, waiting for transfers between devices: 11.1 us -> 6.6 us  [exchange(): return lax.all_to_all(x, AXES, split_axis=0, concat_axis=0, tiled=True)]
  transfers between devices with their start and end apart: 1 -> 1, of which waited for: 1 -> 1; matrix products, arithmetic and copies ran while one was open for 0% -> 0% of each run, Pallas kernels for 10% -> 20%
where the time goes in v2:
time: 99.6 us; the launch traced here: 99.3 us
  Pallas kernels  45.9 us (46%)
  blocking collectives  39.8 us (40%)
  waiting for transfers between devices  6.6 us (7%)
  starting transfers between devices  4.72 us (5%)
  local copies, waits for them, and re-layouts  1.55 us (2%)
    all_to_all x1, blocking collectives, exchange(): return lax.all_to_all(x, AXES, split_axis=0, concat_axis=0, tiled=True)  39.8 us
    pallas_call x1, Pallas kernels, body(): pl.pallas_call(lambda *refs: weight_kernel(capacity, *refs), grid=(hidden...  19.6 us
    pallas_call x1, Pallas kernels, body(): pl.pallas_call(lambda *refs: expert_kernel(capacity, *refs), in_specs=[hb...  18.2 us
    all_to_all x1, waiting for transfers between devices, exchange(): return lax.all_to_all(x, AXES, split_axis=0, concat_axis=0, tiled=True)  6.6 us
    all_to_all x1, starting transfers between devices, exchange(): return lax.all_to_all(x, AXES, split_axis=0, concat_axis=0, tiled=True)  4.72 us
    pallas_call x1, Pallas kernels, body(): pl.pallas_call(lambda *refs: dispatch_kernel(capacity, experts, *refs), i...  4.09 us
    pallas_call x1, Pallas kernels, body(): pl.pallas_call(lambda *refs: combine_kernel(capacity, experts, *refs), ou...  3.46 us
  transfers between devices with their start and end apart: 1, of which 1 were waited for; matrix products, arithmetic and copies ran while one was open for 0% of the time, Pallas kernels for 20%

profile of v2, /device:TPU:1, one launch (start us, length us, event | category | flops | bytes accessed | tf_op | source)
XLA Modules:
  0.0 99.3 jit_solution(3016131940595094025)
XLA Ops:
  0.6 4.1 %shard_map.101 = bf16[128,2,3840]{2,1,0:T(2,128)(2,1)} custom-call(s32[1,512]{1,0:T(1,128)} %bitcast.7, f32[1,512]{1,0:T(1,128)} %bitcast.9, bf16[512,768]{1,0:T(8,128)(2,1)} %refs_2_.2, bf16[512,768]{1,0:T(8,128)(2,1)} %refs_2_.3), custom_call_target="tpu_custom_call" | custom-call | tf_op jit(solution)/shard_map/pallas_call | solution.py:261
  4.7 39.8 %all_to_all.10.refs_0_ = bf16[128,2,3840]{2,1,0:T(2,128)(2,1)} all-to-all(bf16[128,2,3840]{2,1,0:T(2,128)(2,1)} %shard_map.101), channel_id=1, replica_groups=mesh['row'=8,'col'=16] {'row','col'}, dimensions={0} | all-to-all | bytes 3932160 | tf_op jit(solution)/shard_map/all_to_all | solution.py:254
  44.5 0.0 copy-start.2
  44.5 0.0 copy-start.3
  44.5 18.2 %shard_map.102 = bf16[128,2,3840]{2,1,0:T(2,128)(2,1)} custom-call(bf16[128,2,3840]{2,1,0:T(2,128)(2,1)} %all_to_all.10.refs_0_, bf16[768,3072]{1,0:T(8,128)(2,1)} %bitcast.11, bf16[3072,768]{1,0:T(8,128)(2,1)} %bitcast.13), custom_call_target="tpu_custom_call" | custom-call | flops 12079595520 | bytes 13631488 | tf_op jit(solution)/shard_map/pallas_call | solution.py:283
  62.7 4.7 %all-to-all-start.1 = ((bf16[128,2,3840]{2,1,0:T(2,128)(2,1)}), bf16[128,2,3840]{2,1,0:T(2,128)(2,1)S(1)}, u32[]{:S(2)}, u32[]{:S(2)}) async-start(bf16[128,2,3840]{2,1,0:T(2,128)(2,1)} %shard_map.102), calls=%async_computation.1 | async-start | bytes 3932160 | tf_op jit(solution)/shard_map/all_to_all | solution.py:254
  67.5 0.0 copy-done.2
  67.5 0.0 copy-done.3
  67.5 0.5 shard_map.103.refs_1_
  68.0 0.0 copy-start.1
  68.0 1.5 %copy-done.1 = bf16[128,2,3840]{2,1,0:T(2,128)(2,1)S(1)} copy-done((bf16[128,2,3840]{2,1,0:T(2,128)(2,1)S(1)}, bf16[128,2,3840]{2,1,0:T(2,128)(2,1)}, u32[]{:S(2)}) %copy-start.1) | copy-done | bytes 1966104
  69.5 0.0 copy-start
  69.5 19.6 %shard_map.105 = (bf16[768,3072]{1,0:T(8,128)(2,1)}, bf16[3072,768]{1,0:T(8,128)(2,1)}) custom-call(bf16[128,2,3840]{2,1,0:T(2,128)(2,1)S(1)} %copy-done.1, bf16[768,3072]{1,0:T(8,128)(2,1)} %bitcast.12, bf16[3072,768]{1,0:T(8,128)(2,1)} %bitcast.14), custom_call_target="tpu_custom_call" | custom-call | flops 12079595520 | bytes 22020096 | tf_op jit(solution)/shard_map/pallas_call | solution.py:308
  89.2 6.6 %all-to-all-done.1.refs_0_ = bf16[128,2,3840]{2,1,0:T(2,128)(2,1)S(1)} async-done(((bf16[128,2,3840]{2,1,0:T(2,128)(2,1)}), bf16[128,2,3840]{2,1,0:T(2,128)(2,1)S(1)}, u32[]{:S(2)}, u32[]{:S(2)}) %all-to-all-start.1) | async-done | bytes 1966112 | tf_op jit(solution)/shard_map/all_to_all | solution.py:254
  95.8 0.0 copy-done
  95.8 3.5 %shard_map.104 = (bf16[512,768]{1,0:T(8,128)(2,1)}, bf16[512,768]{1,0:T(8,128)(2,1)}, f32[1,512]{1,0:T(1,128)}) custom-call(bf16[128,2,3840]{2,1,0:T(2,128)(2,1)S(1)} %all-to-all-done.1.refs_0_, f32[512,2]{1,0:T(8,128)S(1)} %shard_map.103.refs_1_, bf16[512,768]{1,0:T(8,128)(2,1)S(1)} %copy-done), custom_call_target="tpu_custom_call" | custom-call | tf_op jit(solution)/shard_map/pallas_call | solution.py:320
Async XLA Ops:
  44.5 22.9 %copy-start.2 = (s32[512,1]{0,1:T(1,128)S(1)}, s32[512,1]{0,1:T(1,128)}, u32[]{:S(2)}) copy-start(s32[512,1]{0,1:T(1,128)} %param.7) | copy-start | bytes 6148
  44.5 22.9 %copy-start.3 = (f32[512]{0:T(512)S(1)}, f32[512]{0:T(512)}, u32[]{:S(2)}) copy-start(f32[512]{0:T(512)} %param.8) | copy-start | bytes 6148
  62.7 33.0 %all-to-all-start.1 = ((bf16[128,2,3840]{2,1,0:T(2,128)(2,1)}), bf16[128,2,3840]{2,1,0:T(2,128)(2,1)S(1)}, u32[]{:S(2)}, u32[]{:S(2)}) async-start(bf16[128,2,3840]{2,1,0:T(2,128)(2,1)} %shard_map.102), calls=%async_computation.1 | async-start | bytes 3932160 | tf_op jit(solution)/shard_map/all_to_all | solution.py:254
  68.0 1.6 %copy-start.1 = (bf16[128,2,3840]{2,1,0:T(2,128)(2,1)S(1)}, bf16[128,2,3840]{2,1,0:T(2,128)(2,1)}, u32[]{:S(2)}) copy-start(bf16[128,2,3840]{2,1,0:T(2,128)(2,1)} %all_to_all.10.refs_0_) | copy-start | bytes 5898244
  69.5 26.3 %copy-start = (bf16[512,768]{1,0:T(8,128)(2,1)S(1)}, bf16[512,768]{1,0:T(8,128)(2,1)}, u32[]{:S(2)}) copy-start(bf16[512,768]{1,0:T(8,128)(2,1)} %refs_2_.3) | copy-start | bytes 2359300

commit v3 on v2

--- a/solution.py
+++ b/solution.py
@@ -121,13 +121,11 @@
     return lax.dot_general(a, b, (((0,), (0,)), ((), ())), preferred_element_type=F32)
 
 
-def split_pairs(capacity, pairs_ref, first_ref, second_ref, fetches=None):
+def split_pairs(capacity, pairs_ref, first_ref, second_ref):
     groups = pairs_ref.shape[0]
     width = first_ref.shape[1]
     split = pair_matrix(groups)
     for k in range(capacity):
-        if fetches is not None:
-            fetches[k].wait()
         both = pairs_ref[:, :, k * width : (k + 1) * width].reshape(2 * groups, width)
         both = jnp.dot(split, both, preferred_element_type=F32).astype(BF16)
         here = slice(k * groups, (k + 1) * groups)
@@ -137,10 +135,9 @@
 
 def activate(v, grad_act):
     square = v * v
-    t = jnp.tanh(v * (ROOT + CUBE * square))
-    half = 0.5 * v
-    slope = (0.5 + 0.5 * t) + (half * (ROOT + 3.0 * CUBE * square)) * (1.0 - t * t)
-    return (half + half * t).astype(BF16), (grad_act * slope).astype(BF16)
+    w = 0.5 + 0.5 * jnp.tanh(v * (ROOT + CUBE * square))
+    r = v * (2.0 * ROOT + 6.0 * CUBE * square)
+    return (v * w).astype(BF16), ((grad_act * w) * (1.0 + (1.0 - w) * r)).astype(BF16)
 
 
 def expert_kernel(
@@ -179,10 +176,12 @@
     for pair in fetches[:1]:
         for fetch in pair:
             fetch.start()
-    split_pairs(capacity, sent_ref, rows_ref, cots_ref, arrivals)
+    for fetch in arrivals:
+        fetch.wait()
     for pair in fetches[1:]:
         for fetch in pair:
             fetch.start()
+    split_pairs(capacity, sent_ref, rows_ref, cots_ref)
     for c, here in enumerate(parts):
         for pair in fetches[c : c + 1] if c < 2 else fetches[2:] if c == 2 else []:
             for fetch in pair:

time: 99.6 us -> 99.2 us (level)
  no operation moved by 1% of the time
where the time goes in v3:
time: 99.2 us; the launch traced here: 98.8 us
  Pallas kernels  45.1 us (45%)
  blocking collectives  39.8 us (40%)
  waiting for transfers between devices  6.98 us (7%)
  starting transfers between devices  4.75 us (5%)
  local copies, waits for them, and re-layouts  1.55 us (2%)
    all_to_all x1, blocking collectives, exchange(): return lax.all_to_all(x, AXES, split_axis=0, concat_axis=0, tiled=True)  39.8 us
    pallas_call x1, Pallas kernels, body(): pl.pallas_call(lambda *refs: weight_kernel(capacity, *refs), grid=(hidden...  19.3 us
    pallas_call x1, Pallas kernels, body(): pl.pallas_call(lambda *refs: expert_kernel(capacity, *refs), in_specs=[hb...  17.8 us
    all_to_all x1, waiting for transfers between devices, exchange(): return lax.all_to_all(x, AXES, split_axis=0, concat_axis=0, tiled=True)  6.98 us
    all_to_all x1, starting transfers between devices, exchange(): return lax.all_to_all(x, AXES, split_axis=0, concat_axis=0, tiled=True)  4.75 us
    pallas_call x1, Pallas kernels, body(): pl.pallas_call(lambda *refs: dispatch_kernel(capacity, experts, *refs), i...  4.09 us
    pallas_call x1, Pallas kernels, body(): pl.pallas_call(lambda *refs: combine_kernel(capacity, experts, *refs), ou...  3.46 us
  transfers between devices with their start and end apart: 1, of which 1 were waited for; matrix products, arithmetic and copies ran while one was open for 0% of the time, Pallas kernels for 20%

profile of v3, /device:TPU:1, one launch (start us, length us, event | category | flops | bytes accessed | tf_op | source)
XLA Modules:
  0.0 98.8 jit_solution(8134813350608539206)
XLA Ops:
  0.6 4.1 %shard_map.101 = bf16[128,2,3840]{2,1,0:T(2,128)(2,1)} custom-call(s32[1,512]{1,0:T(1,128)} %bitcast.7, f32[1,512]{1,0:T(1,128)} %bitcast.9, bf16[512,768]{1,0:T(8,128)(2,1)} %refs_2_.2, bf16[512,768]{1,0:T(8,128)(2,1)} %refs_2_.3), custom_call_target="tpu_custom_call" | custom-call | tf_op jit(solution)/shard_map/pallas_call | solution.py:260
  4.7 39.8 %all_to_all.10.refs_0_ = bf16[128,2,3840]{2,1,0:T(2,128)(2,1)} all-to-all(bf16[128,2,3840]{2,1,0:T(2,128)(2,1)} %shard_map.101), channel_id=1, replica_groups=mesh['row'=8,'col'=16] {'row','col'}, dimensions={0} | all-to-all | bytes 3932160 | tf_op jit(solution)/shard_map/all_to_all | solution.py:253
  44.5 0.0 copy-start.2
  44.5 0.0 copy-start.3
  44.5 17.8 %shard_map.102 = bf16[128,2,3840]{2,1,0:T(2,128)(2,1)} custom-call(bf16[128,2,3840]{2,1,0:T(2,128)(2,1)} %all_to_all.10.refs_0_, bf16[768,3072]{1,0:T(8,128)(2,1)} %bitcast.11, bf16[3072,768]{1,0:T(8,128)(2,1)} %bitcast.13), custom_call_target="tpu_custom_call" | custom-call | flops 12079595520 | bytes 13631488 | tf_op jit(solution)/shard_map/pallas_call | solution.py:282
  62.3 4.7 %all-to-all-start.1 = ((bf16[128,2,3840]{2,1,0:T(2,128)(2,1)}), bf16[128,2,3840]{2,1,0:T(2,128)(2,1)S(1)}, u32[]{:S(2)}, u32[]{:S(2)}) async-start(bf16[128,2,3840]{2,1,0:T(2,128)(2,1)} %shard_map.102), calls=%async_computation.1 | async-start | bytes 3932160 | tf_op jit(solution)/shard_map/all_to_all | solution.py:253
  67.0 0.0 copy-done.2
  67.1 0.0 copy-done.3
  67.1 0.5 shard_map.103.refs_1_
  67.6 0.0 copy-start.1
  67.6 1.5 %copy-done.1 = bf16[128,2,3840]{2,1,0:T(2,128)(2,1)S(1)} copy-done((bf16[128,2,3840]{2,1,0:T(2,128)(2,1)S(1)}, bf16[128,2,3840]{2,1,0:T(2,128)(2,1)}, u32[]{:S(2)}) %copy-start.1) | copy-done | bytes 1966104
  69.1 0.0 copy-start
  69.1 19.3 %shard_map.105 = (bf16[768,3072]{1,0:T(8,128)(2,1)}, bf16[3072,768]{1,0:T(8,128)(2,1)}) custom-call(bf16[128,2,3840]{2,1,0:T(2,128)(2,1)S(1)} %copy-done.1, bf16[768,3072]{1,0:T(8,128)(2,1)} %bitcast.12, bf16[3072,768]{1,0:T(8,128)(2,1)} %bitcast.14), custom_call_target="tpu_custom_call" | custom-call | flops 12079595520 | bytes 22020096 | tf_op jit(solution)/shard_map/pallas_call | solution.py:307
  88.4 7.0 %all-to-all-done.1.refs_0_ = bf16[128,2,3840]{2,1,0:T(2,128)(2,1)S(1)} async-done(((bf16[128,2,3840]{2,1,0:T(2,128)(2,1)}), bf16[128,2,3840]{2,1,0:T(2,128)(2,1)S(1)}, u32[]{:S(2)}, u32[]{:S(2)}) %all-to-all-start.1) | async-done | bytes 1966112 | tf_op jit(solution)/shard_map/all_to_all | solution.py:253
  95.4 0.0 copy-done
  95.4 3.5 %shard_map.104 = (bf16[512,768]{1,0:T(8,128)(2,1)}, bf16[512,768]{1,0:T(8,128)(2,1)}, f32[1,512]{1,0:T(1,128)}) custom-call(bf16[128,2,3840]{2,1,0:T(2,128)(2,1)S(1)} %all-to-all-done.1.refs_0_, f32[512,2]{1,0:T(8,128)S(1)} %shard_map.103.refs_1_, bf16[512,768]{1,0:T(8,128)(2,1)S(1)} %copy-done), custom_call_target="tpu_custom_call" | custom-call | tf_op jit(solution)/shard_map/pallas_call | solution.py:319
Async XLA Ops:
  44.5 22.5 %copy-start.2 = (s32[512,1]{0,1:T(1,128)S(1)}, s32[512,1]{0,1:T(1,128)}, u32[]{:S(2)}) copy-start(s32[512,1]{0,1:T(1,128)} %param.7) | copy-start | bytes 6148
  44.5 22.5 %copy-start.3 = (f32[512]{0:T(512)S(1)}, f32[512]{0:T(512)}, u32[]{:S(2)}) copy-start(f32[512]{0:T(512)} %param.8) | copy-start | bytes 6148
  62.3 33.1 %all-to-all-start.1 = ((bf16[128,2,3840]{2,1,0:T(2,128)(2,1)}), bf16[128,2,3840]{2,1,0:T(2,128)(2,1)S(1)}, u32[]{:S(2)}, u32[]{:S(2)}) async-start(bf16[128,2,3840]{2,1,0:T(2,128)(2,1)} %shard_map.102), calls=%async_computation.1 | async-start | bytes 3932160 | tf_op jit(solution)/shard_map/all_to_all | solution.py:253
  67.6 1.6 %copy-start.1 = (bf16[128,2,3840]{2,1,0:T(2,128)(2,1)S(1)}, bf16[128,2,3840]{2,1,0:T(2,128)(2,1)}, u32[]{:S(2)}) copy-start(bf16[128,2,3840]{2,1,0:T(2,128)(2,1)} %all_to_all.10.refs_0_) | copy-start | bytes 5898244
  69.1 26.3 %copy-start = (bf16[512,768]{1,0:T(8,128)(2,1)S(1)}, bf16[512,768]{1,0:T(8,128)(2,1)}, u32[]{:S(2)}) copy-start(bf16[512,768]{1,0:T(8,128)(2,1)} %refs_2_.3) | copy-start | bytes 2359300

commit v4 on v3

--- a/solution.py
+++ b/solution.py
@@ -98,10 +98,11 @@
     code = slot_code_row(ids_ref[...], capacity, experts)
     slot = lax.broadcasted_iota(jnp.int32, (experts * capacity, 1), 0)
     pick = (code == slot).astype(F32).astype(BF16)
-    for fetch in fetches[1:]:
-        fetch.wait()
+    fetches[2].wait()
+    rows = jnp.dot(pick, tokens_ref[...], preferred_element_type=F32).astype(BF16)
+    fetches[1].wait()
     gate = as_column(gate_ref[...])
-    rows = jnp.dot(pick, tokens_ref[...], preferred_element_type=F32).astype(BF16)
+    fetches[3].wait()
     scaled = (gate * cot_ref[...].astype(F32)).astype(BF16)
     cots = jnp.dot(pick, scaled, preferred_element_type=F32).astype(BF16)
     join_pairs(capacity, rows, cots, out_ref, out_hbm, sems)

time: 99.2 us -> 99.6 us (level)
  no operation moved by 1% of the time
where the time goes in v4:
time: 99.6 us; the launch traced here: 99.2 us
  Pallas kernels  45.5 us (46%)
  blocking collectives  39.8 us (40%)
  waiting for transfers between devices  6.98 us (7%)
  starting transfers between devices  4.73 us (5%)
  local copies, waits for them, and re-layouts  1.55 us (2%)
    all_to_all x1, blocking collectives, exchange(): return lax.all_to_all(x, AXES, split_axis=0, concat_axis=0, tiled=True)  39.8 us
    pallas_call x1, Pallas kernels, body(): pl.pallas_call(lambda *refs: weight_kernel(capacity, *refs), grid=(hidden...  19.3 us
    pallas_call x1, Pallas kernels, body(): pl.pallas_call(lambda *refs: expert_kernel(capacity, *refs), in_specs=[hb...  17.8 us
    all_to_all x1, waiting for transfers between devices, exchange(): return lax.all_to_all(x, AXES, split_axis=0, concat_axis=0, tiled=True)  6.98 us
    all_to_all x1, starting transfers between devices, exchange(): return lax.all_to_all(x, AXES, split_axis=0, concat_axis=0, tiled=True)  4.73 us
    pallas_call x1, Pallas kernels, body(): pl.pallas_call(lambda *refs: dispatch_kernel(capacity, experts, *refs), i...  4.49 us
    pallas_call x1, Pallas kernels, body(): pl.pallas_call(lambda *refs: combine_kernel(capacity, experts, *refs), ou...  3.46 us
  transfers between devices with their start and end apart: 1, of which 1 were waited for; matrix products, arithmetic and copies ran while one was open for 0% of the time, Pallas kernels for 20%

profile of v4, /device:TPU:1, one launch (start us, length us, event | category | flops | bytes accessed | tf_op | source)
XLA Modules:
  0.0 99.2 jit_solution(14367801184579466293)
XLA Ops:
  0.6 4.5 %shard_map.101 = bf16[128,2,3840]{2,1,0:T(2,128)(2,1)} custom-call(s32[1,512]{1,0:T(1,128)} %bitcast.7, f32[1,512]{1,0:T(1,128)} %bitcast.9, bf16[512,768]{1,0:T(8,128)(2,1)} %refs_2_.2, bf16[512,768]{1,0:T(8,128)(2,1)} %refs_2_.3), custom_call_target="tpu_custom_call" | custom-call | tf_op jit(solution)/shard_map/pallas_call | solution.py:261
  5.1 39.8 %all_to_all.10.refs_0_ = bf16[128,2,3840]{2,1,0:T(2,128)(2,1)} all-to-all(bf16[128,2,3840]{2,1,0:T(2,128)(2,1)} %shard_map.101), channel_id=1, replica_groups=mesh['row'=8,'col'=16] {'row','col'}, dimensions={0} | all-to-all | bytes 3932160 | tf_op jit(solution)/shard_map/all_to_all | solution.py:254
  44.9 0.0 copy-start.2
  44.9 0.0 copy-start.3
  44.9 17.8 %shard_map.102 = bf16[128,2,3840]{2,1,0:T(2,128)(2,1)} custom-call(bf16[128,2,3840]{2,1,0:T(2,128)(2,1)} %all_to_all.10.refs_0_, bf16[768,3072]{1,0:T(8,128)(2,1)} %bitcast.11, bf16[3072,768]{1,0:T(8,128)(2,1)} %bitcast.13), custom_call_target="tpu_custom_call" | custom-call | flops 12079595520 | bytes 13631488 | tf_op jit(solution)/shard_map/pallas_call | solution.py:283
  62.7 4.7 %all-to-all-start.1 = ((bf16[128,2,3840]{2,1,0:T(2,128)(2,1)}), bf16[128,2,3840]{2,1,0:T(2,128)(2,1)S(1)}, u32[]{:S(2)}, u32[]{:S(2)}) async-start(bf16[128,2,3840]{2,1,0:T(2,128)(2,1)} %shard_map.102), calls=%async_computation.1 | async-start | bytes 3932160 | tf_op jit(solution)/shard_map/all_to_all | solution.py:254
  67.4 0.0 copy-done.2
  67.4 0.0 copy-done.3
  67.5 0.5 shard_map.103.refs_1_
  68.0 0.0 copy-start.1
  68.0 1.5 %copy-done.1 = bf16[128,2,3840]{2,1,0:T(2,128)(2,1)S(1)} copy-done((bf16[128,2,3840]{2,1,0:T(2,128)(2,1)S(1)}, bf16[128,2,3840]{2,1,0:T(2,128)(2,1)}, u32[]{:S(2)}) %copy-start.1) | copy-done | bytes 1966104
  69.5 0.0 copy-start
  69.5 19.3 %shard_map.105 = (bf16[768,3072]{1,0:T(8,128)(2,1)}, bf16[3072,768]{1,0:T(8,128)(2,1)}) custom-call(bf16[128,2,3840]{2,1,0:T(2,128)(2,1)S(1)} %copy-done.1, bf16[768,3072]{1,0:T(8,128)(2,1)} %bitcast.12, bf16[3072,768]{1,0:T(8,128)(2,1)} %bitcast.14), custom_call_target="tpu_custom_call" | custom-call | flops 12079595520 | bytes 22020096 | tf_op jit(solution)/shard_map/pallas_call | solution.py:308
  88.8 7.0 %all-to-all-done.1.refs_0_ = bf16[128,2,3840]{2,1,0:T(2,128)(2,1)S(1)} async-done(((bf16[128,2,3840]{2,1,0:T(2,128)(2,1)}), bf16[128,2,3840]{2,1,0:T(2,128)(2,1)S(1)}, u32[]{:S(2)}, u32[]{:S(2)}) %all-to-all-start.1) | async-done | bytes 1966112 | tf_op jit(solution)/shard_map/all_to_all | solution.py:254
  95.8 0.0 copy-done
  95.8 3.5 %shard_map.104 = (bf16[512,768]{1,0:T(8,128)(2,1)}, bf16[512,768]{1,0:T(8,128)(2,1)}, f32[1,512]{1,0:T(1,128)}) custom-call(bf16[128,2,3840]{2,1,0:T(2,128)(2,1)S(1)} %all-to-all-done.1.refs_0_, f32[512,2]{1,0:T(8,128)S(1)} %shard_map.103.refs_1_, bf16[512,768]{1,0:T(8,128)(2,1)S(1)} %copy-done), custom_call_target="tpu_custom_call" | custom-call | tf_op jit(solution)/shard_map/pallas_call | solution.py:320
Async XLA Ops:
  44.9 22.5 %copy-start.2 = (s32[512,1]{0,1:T(1,128)S(1)}, s32[512,1]{0,1:T(1,128)}, u32[]{:S(2)}) copy-start(s32[512,1]{0,1:T(1,128)} %param.7) | copy-start | bytes 6148
  44.9 22.5 %copy-start.3 = (f32[512]{0:T(512)S(1)}, f32[512]{0:T(512)}, u32[]{:S(2)}) copy-start(f32[512]{0:T(512)} %param.8) | copy-start | bytes 6148
  62.7 33.1 %all-to-all-start.1 = ((bf16[128,2,3840]{2,1,0:T(2,128)(2,1)}), bf16[128,2,3840]{2,1,0:T(2,128)(2,1)S(1)}, u32[]{:S(2)}, u32[]{:S(2)}) async-start(bf16[128,2,3840]{2,1,0:T(2,128)(2,1)} %shard_map.102), calls=%async_computation.1 | async-start | bytes 3932160 | tf_op jit(solution)/shard_map/all_to_all | solution.py:254
  68.0 1.6 %copy-start.1 = (bf16[128,2,3840]{2,1,0:T(2,128)(2,1)S(1)}, bf16[128,2,3840]{2,1,0:T(2,128)(2,1)}, u32[]{:S(2)}) copy-start(bf16[128,2,3840]{2,1,0:T(2,128)(2,1)} %all_to_all.10.refs_0_) | copy-start | bytes 5898244
  69.5 26.3 %copy-start = (bf16[512,768]{1,0:T(8,128)(2,1)S(1)}, bf16[512,768]{1,0:T(8,128)(2,1)}, u32[]{:S(2)}) copy-start(bf16[512,768]{1,0:T(8,128)(2,1)} %refs_2_.3) | copy-start | bytes 2359300

commit v5 on v3

--- a/solution.py
+++ b/solution.py
@@ -94,12 +94,11 @@
     ]
     for fetch in fetches:
         fetch.start()
-    fetches[0].wait()
+    for fetch in fetches:
+        fetch.wait()
     code = slot_code_row(ids_ref[...], capacity, experts)
     slot = lax.broadcasted_iota(jnp.int32, (experts * capacity, 1), 0)
     pick = (code == slot).astype(F32).astype(BF16)
-    for fetch in fetches[1:]:
-        fetch.wait()
     gate = as_column(gate_ref[...])
     rows = jnp.dot(pick, tokens_ref[...], preferred_element_type=F32).astype(BF16)
     scaled = (gate * cot_ref[...].astype(F32)).astype(BF16)

time: 99.2 us -> 99.4 us (level)
  no operation moved by 1% of the time
where the time goes in v5:
time: 99.4 us; the launch traced here: 99 us
  Pallas kernels  45.3 us (46%)
  blocking collectives  39.8 us (40%)
  waiting for transfers between devices  6.98 us (7%)
  starting transfers between devices  4.74 us (5%)
  local copies, waits for them, and re-layouts  1.55 us (2%)
    all_to_all x1, blocking collectives, exchange(): return lax.all_to_all(x, AXES, split_axis=0, concat_axis=0, tiled=True)  39.8 us
    pallas_call x1, Pallas kernels, body(): pl.pallas_call(lambda *refs: weight_kernel(capacity, *refs), grid=(hidden...  19.3 us
    pallas_call x1, Pallas kernels, body(): pl.pallas_call(lambda *refs: expert_kernel(capacity, *refs), in_specs=[hb...  17.8 us
    all_to_all x1, waiting for transfers between devices, exchange(): return lax.all_to_all(x, AXES, split_axis=0, concat_axis=0, tiled=True)  6.98 us
    all_to_all x1, starting transfers between devices, exchange(): return lax.all_to_all(x, AXES, split_axis=0, concat_axis=0, tiled=True)  4.74 us
    pallas_call x1, Pallas kernels, body(): pl.pallas_call(lambda *refs: dispatch_kernel(capacity, experts, *refs), i...  4.29 us
    pallas_call x1, Pallas kernels, body(): pl.pallas_call(lambda *refs: combine_kernel(capacity, experts, *refs), ou...  3.46 us
  transfers between devices with their start and end apart: 1, of which 1 were waited for; matrix products, arithmetic and copies ran while one was open for 0% of the time, Pallas kernels for 20%

profile of v5, /device:TPU:1, one launch (start us, length us, event | category | flops | bytes accessed | tf_op | source)
XLA Modules:
  0.0 99.0 jit_solution(5543828430974657576)
XLA Ops:
  0.6 4.3 %shard_map.101 = bf16[128,2,3840]{2,1,0:T(2,128)(2,1)} custom-call(s32[1,512]{1,0:T(1,128)} %bitcast.7, f32[1,512]{1,0:T(1,128)} %bitcast.9, bf16[512,768]{1,0:T(8,128)(2,1)} %refs_2_.2, bf16[512,768]{1,0:T(8,128)(2,1)} %refs_2_.3), custom_call_target="tpu_custom_call" | custom-call | tf_op jit(solution)/shard_map/pallas_call | solution.py:259
  4.9 39.8 %all_to_all.10.refs_0_ = bf16[128,2,3840]{2,1,0:T(2,128)(2,1)} all-to-all(bf16[128,2,3840]{2,1,0:T(2,128)(2,1)} %shard_map.101), channel_id=1, replica_groups=mesh['row'=8,'col'=16] {'row','col'}, dimensions={0} | all-to-all | bytes 3932160 | tf_op jit(solution)/shard_map/all_to_all | solution.py:252
  44.7 0.0 copy-start.2
  44.7 0.0 copy-start.3
  44.7 17.8 %shard_map.102 = bf16[128,2,3840]{2,1,0:T(2,128)(2,1)} custom-call(bf16[128,2,3840]{2,1,0:T(2,128)(2,1)} %all_to_all.10.refs_0_, bf16[768,3072]{1,0:T(8,128)(2,1)} %bitcast.11, bf16[3072,768]{1,0:T(8,128)(2,1)} %bitcast.13), custom_call_target="tpu_custom_call" | custom-call | flops 12079595520 | bytes 13631488 | tf_op jit(solution)/shard_map/pallas_call | solution.py:281
  62.5 4.7 %all-to-all-start.1 = ((bf16[128,2,3840]{2,1,0:T(2,128)(2,1)}), bf16[128,2,3840]{2,1,0:T(2,128)(2,1)S(1)}, u32[]{:S(2)}, u32[]{:S(2)}) async-start(bf16[128,2,3840]{2,1,0:T(2,128)(2,1)} %shard_map.102), calls=%async_computation.1 | async-start | bytes 3932160 | tf_op jit(solution)/shard_map/all_to_all | solution.py:252
  67.2 0.0 copy-done.2
  67.3 0.0 copy-done.3
  67.3 0.5 shard_map.103.refs_1_
  67.8 0.0 copy-start.1
  67.8 1.5 %copy-done.1 = bf16[128,2,3840]{2,1,0:T(2,128)(2,1)S(1)} copy-done((bf16[128,2,3840]{2,1,0:T(2,128)(2,1)S(1)}, bf16[128,2,3840]{2,1,0:T(2,128)(2,1)}, u32[]{:S(2)}) %copy-start.1) | copy-done | bytes 1966104
  69.3 0.0 copy-start
  69.3 19.3 %shard_map.105 = (bf16[768,3072]{1,0:T(8,128)(2,1)}, bf16[3072,768]{1,0:T(8,128)(2,1)}) custom-call(bf16[128,2,3840]{2,1,0:T(2,128)(2,1)S(1)} %copy-done.1, bf16[768,3072]{1,0:T(8,128)(2,1)} %bitcast.12, bf16[3072,768]{1,0:T(8,128)(2,1)} %bitcast.14), custom_call_target="tpu_custom_call" | custom-call | flops 12079595520 | bytes 22020096 | tf_op jit(solution)/shard_map/pallas_call | solution.py:306
  88.6 7.0 %all-to-all-done.1.refs_0_ = bf16[128,2,3840]{2,1,0:T(2,128)(2,1)S(1)} async-done(((bf16[128,2,3840]{2,1,0:T(2,128)(2,1)}), bf16[128,2,3840]{2,1,0:T(2,128)(2,1)S(1)}, u32[]{:S(2)}, u32[]{:S(2)}) %all-to-all-start.1) | async-done | bytes 1966112 | tf_op jit(solution)/shard_map/all_to_all | solution.py:252
  95.6 0.0 copy-done
  95.6 3.5 %shard_map.104 = (bf16[512,768]{1,0:T(8,128)(2,1)}, bf16[512,768]{1,0:T(8,128)(2,1)}, f32[1,512]{1,0:T(1,128)}) custom-call(bf16[128,2,3840]{2,1,0:T(2,128)(2,1)S(1)} %all-to-all-done.1.refs_0_, f32[512,2]{1,0:T(8,128)S(1)} %shard_map.103.refs_1_, bf16[512,768]{1,0:T(8,128)(2,1)S(1)} %copy-done), custom_call_target="tpu_custom_call" | custom-call | tf_op jit(solution)/shard_map/pallas_call | solution.py:318
Async XLA Ops:
  44.7 22.5 %copy-start.2 = (s32[512,1]{0,1:T(1,128)S(1)}, s32[512,1]{0,1:T(1,128)}, u32[]{:S(2)}) copy-start(s32[512,1]{0,1:T(1,128)} %param.7) | copy-start | bytes 6148
  44.7 22.5 %copy-start.3 = (f32[512]{0:T(512)S(1)}, f32[512]{0:T(512)}, u32[]{:S(2)}) copy-start(f32[512]{0:T(512)} %param.8) | copy-start | bytes 6148
  62.5 33.1 %all-to-all-start.1 = ((bf16[128,2,3840]{2,1,0:T(2,128)(2,1)}), bf16[128,2,3840]{2,1,0:T(2,128)(2,1)S(1)}, u32[]{:S(2)}, u32[]{:S(2)}) async-start(bf16[128,2,3840]{2,1,0:T(2,128)(2,1)} %shard_map.102), calls=%async_computation.1 | async-start | bytes 3932160 | tf_op jit(solution)/shard_map/all_to_all | solution.py:252
  67.8 1.6 %copy-start.1 = (bf16[128,2,3840]{2,1,0:T(2,128)(2,1)S(1)}, bf16[128,2,3840]{2,1,0:T(2,128)(2,1)}, u32[]{:S(2)}) copy-start(bf16[128,2,3840]{2,1,0:T(2,128)(2,1)} %all_to_all.10.refs_0_) | copy-start | bytes 5898244
  69.3 26.3 %copy-start = (bf16[512,768]{1,0:T(8,128)(2,1)S(1)}, bf16[512,768]{1,0:T(8,128)(2,1)}, u32[]{:S(2)}) copy-start(bf16[512,768]{1,0:T(8,128)(2,1)} %refs_2_.3) | copy-start | bytes 2359300
